TPU v7x, 256 devices: a whole 4x4x8 slice. The times are simulated.
256 devices in a mesh: gz: 64 (over z, x, core), col: 4 (over y).
Axes of the slice: x: 4, y: 4, z: 8, core: 2. Of those that a mesh axis runs over, the one named last changes fastest.
Arguments:
- measured: float32 [736, 65536], P('col', 'gz'), may hold values from -6 to 6
- view_offset: int32 [1024], P('gz'), may hold values from 0 to 224, as said below
- tile_index: int32 [1024], P('gz'), may hold values from 0 to 7
- footprint: float32 [8, 64, 32], replicated, may hold values from -1 to 1
- transaxial: float32 [8, 736, 1024], P(None, 'col'), may hold values from -0.1875 to 0.1875
Outputs:
- volume: float32 [8192, 1024], P('gz', 'col')
- residual: float32 [736, 65536], P('col', 'gz')
- gradient: float32 [8192, 1024], P('gz', 'col')
Inputs may be any that keep to these rules, and one draw needn't show every extreme that they name: `view_offset`: within each block of 16 views the offsets never fall; the block's first view has 0 and its last view has 224.
All inputs are finite; a program needn't handle non-finite values.
Results may differ from a plain program's by a relative error of at most 0.0003.
Values sent between devices are 32-bit elements; how exact they have to be, the bound alone decides.
A program may use at most 64 MiB of HBM per device.

v0:
```python
import functools

import jax
import jax.numpy as jnp
from jax import lax
from jax.experimental import pallas as pl
from jax.experimental.pallas import tpu as pltpu
from jax.sharding import PartitionSpec as P

MESH = pl.DeviceIdType.MESH
F32 = jnp.float32
BF16 = jnp.bfloat16

NA = 8
R = 64
ZW = 32
ZS = 128
HR = 64
WZ = 256
C = 184
NXW = 1024
NCOL = 4
VX = NXW // NCOL
PAIRS = NA // 2
PW = 384
KC = PAIRS * PW
TOP = WZ - ZW
SCALE = 2.0**40
NT = (((1,), (1,)), ((), ()))
NN = (((1,), (0,)), ((), ()))


def split(x):
    hi = x.astype(BF16)
    return hi, (x - hi.astype(F32)).astype(BF16)


def dot(a, b, dims):
    return lax.dot_general(a, b, dimension_numbers=dims, preferred_element_type=F32)


def dot3(a_hi, a_lo, b_hi, b_lo, dims):
    a = jnp.concatenate([a_hi, a_lo, a_hi], axis=dims[0][0][0])
    b = jnp.concatenate([b_hi, b_hi, b_lo], axis=dims[0][1][0])
    return dot(a, b, dims)


def squares(x):
    rows, lanes = x.shape
    y = jnp.sum((x * x).reshape(rows // 8, 8, lanes), axis=0)
    return sum(y[:, k * 128 : (k + 1) * 128] for k in range(lanes // 128))


def total(x):
    return jnp.sum(x, axis=(0, 1), keepdims=True)


def kernel(
    lo_size,
    off_ref, tile_ref, foot_ref, measured_ref, trans_ref,
    vol_ref, res_ref, grad_ref,
    stage, t_hi, t_lo, shifted, w_hi, w_lo,
    z_both, q_all, q0, q1, r1,
    part, rim, direct,
    window, g0, g1, h0, h1, scalars,
    ar1, ar2,
    meas_ref, m_sem, t_sem, rim_send, rim_recv, dir_send, dir_recv,
    gat_send, gat_recv, win_send, win_recv, ar_send, ar_recv,
):
    n_gz = lax.axis_size("gz")
    hi_size = n_gz // lo_size
    x_size = lo_size // 2
    gz = lax.axis_index("gz")
    y = lax.axis_index("col")
    z_at = lax.div(gz, lo_size)
    x_at = lax.div(lax.rem(gz, lo_size), 2)
    core = lax.rem(gz, 2)
    inner, outer = 1 - core, core

    def col(d):
        return lax.rem(y + d, NCOL)

    def flat_peer(d):
        at = lax.rem(x_at * NCOL + y + d, x_size * NCOL)
        return (z_at * lo_size + lax.div(at, NCOL) * 2 + core, lax.rem(at, NCOL))

    def deep_peer(d):
        at = lax.rem(z_at * 2 + core + d, hi_size * 2)
        return (lax.div(at, 2) * lo_size + x_at * 2 + lax.rem(at, 2), y)

    groups = ((x_size * NCOL, flat_peer), (hi_size * 2, deep_peer))

    barrier = pltpu.get_barrier_semaphore()

    def greet(to):
        pl.semaphore_signal(barrier, inc=1, device_id=to, device_id_type=MESH)

    def owner(i):
        return lax.rem(y + 2 + 3 * i + 3 * lax.div(i * (i - 1), 2), NCOL)

    def t_load(i):
        cols = pl.ds(pl.multiple_of(owner(i) * VX, VX), VX)
        return pltpu.make_async_copy(trans_ref.at[:, :, cols], stage.at[i], t_sem.at[i])

    loads = [t_load(i) for i in range(NCOL)]
    meas_load = pltpu.make_async_copy(measured_ref, meas_ref, m_sem)
    meas_load.start()
    for load in loads:
        load.start()

    for other in (1, n_gz - 1):
        greet((lax.rem(gz + other, n_gz), y))
        greet((lax.rem(gz + other, n_gz), col(2)))
    for size, peer in groups:
        for d in range(1, size):
            greet(peer(d))
    greeted = groups[0][0] + groups[1][0] + 2

    lane = lax.broadcasted_iota(jnp.int32, (1, 128), 1)
    first_half = lane < 64

    shifted[...] = jnp.zeros_like(shifted)

    def place(a, _):
        shifted[TOP:WZ, :] = jnp.concatenate(
            [foot_ref[tile_ref[a]], foot_ref[tile_ref[a + NA]]], axis=1
        )
        one = shifted[pl.ds(TOP - off_ref[a], WZ), :]
        two = shifted[pl.ds(TOP - off_ref[a + NA], WZ), :]
        hi, lo = split(jnp.where(first_half, one, two))
        w_hi[a] = hi
        w_lo[a] = lo
        return 0

    lax.fori_loop(0, NA, place, 0)

    def z_of(p, x):
        hi, lo = split(x)
        pick = lambda v, k: jnp.concatenate([v[k * 128 : (k + 1) * 128], v[256:]], axis=0)
        za = dot3(w_hi[2 * p], w_lo[2 * p], pick(hi, 0), pick(lo, 0), NT)
        zb = dot3(w_hi[2 * p + 1], w_lo[2 * p + 1], pick(hi, 1), pick(lo, 1), NT)
        third = jnp.where(first_half, za[:, 128:], zb[:, 128:])
        hi, lo = split(jnp.concatenate([za[:, :128], zb[:, :128], third], axis=1))
        at = pl.ds(pl.multiple_of(p * PW, 128), PW)
        z_both[0:WZ, at] = hi
        z_both[WZ:, at] = lo

    def early_at(p):
        return pl.ds(pl.multiple_of(p * 128, 128), 128)

    def late_at(p):
        return pl.ds(pl.multiple_of(NA * R + p * 128, 128), 128)

    def z_of_measured(p, _):
        early = meas_ref[:, early_at(p)]
        late = meas_ref[:, late_at(p)]
        a = jnp.where(first_half, early, pltpu.roll(late, 64, 1))
        b = jnp.where(first_half, pltpu.roll(early, 64, 1), late)
        gap = jnp.zeros((8, 128), F32)
        z_of(p, jnp.concatenate([a[:128], b[:128], a[128:], gap, b[128:], gap], axis=0))
        return 0

    def as_measured(x):
        a = jnp.concatenate([x[0:128], x[256:312]], axis=0)
        b = jnp.concatenate([x[128:256], x[320:376]], axis=0)
        early = jnp.where(first_half, a, pltpu.roll(b, 64, 1))
        late = jnp.where(first_half, pltpu.roll(a, 64, 1), b)
        return early, late

    meas_load.wait()
    lax.fori_loop(0, PAIRS, z_of_measured, 0, unroll=2)

    def convert(i, s):
        t_load(i).wait()

        def some(p, _):
            base = p * PW
            for h in range(2):
                x = stage[i, 2 * p + h]
                hi, lo = split(x[:128])
                at = pl.ds(pl.multiple_of(base + h * 128, 64), 128)
                t_hi[s, at] = hi
                t_lo[s, at] = lo
                hi, lo = split(jnp.concatenate([x[128:], jnp.zeros((8, VX), F32)], axis=0))
                at = pl.ds(pl.multiple_of(base + 256 + h * 64, 64), 64)
                t_hi[s, at] = hi
                t_lo[s, at] = lo
            return 0

        lax.fori_loop(0, PAIRS, some, 0)

    pl.semaphore_wait(barrier, greeted)

    def remote(src, dst, send, recv, to):
        return pltpu.make_async_remote_copy(
            src_ref=src, dst_ref=dst, send_sem=send, recv_sem=recv, device_id=to, device_id_type=MESH
        )

    ar_bufs = (ar1, ar2)
    ar_at = (x_at * NCOL + y, z_at * 2 + core)

    def ar_put(k, level, value):
        size, peer = groups[level]
        slot = ar_bufs[level].at[k, ar_at[level]]
        slot[...] = value
        for d in range(1, size):
            remote(slot, slot, ar_send.at[k, level], ar_recv.at[k, level], peer(d)).start()

    def ar_get(k, level):
        size, peer = groups[level]
        others = ar_bufs[level].at[k, pl.ds(0, size - 1)]
        every = remote(others, others, ar_send.at[k, level], ar_recv.at[k, level], peer(1))
        every.wait_recv()
        every.wait_send()
        return jnp.sum(ar_bufs[level][k], axis=0)

    def ar_first(k, one, two):
        rows = [jnp.sum(v, axis=0, keepdims=True) for v in (one, two)]
        ar_put(k, 0, jnp.concatenate(rows, axis=0))

    def ar_second(k):
        ar_put(k, 1, ar_get(k, 0))

    def half(h, base=HR):
        return pl.ds(pl.multiple_of(base + h * 64, 64), 64)

    def edge(h):
        return pl.ds(pl.multiple_of((1 - h) * (WZ - HR), 64), HR)

    def b_rim(phase, i, h):
        return remote(
            part.at[phase, i, edge(h)], rim.at[phase, i, h],
            rim_send.at[phase, i, h], rim_recv.at[phase, i, h],
            (lax.rem(gz + n_gz + 1 - 2 * h, n_gz), y),
        )

    def b_direct(phase, i, h):
        return remote(
            part.at[phase, i, half(h)], direct.at[phase, i, half(h, 0)],
            dir_send.at[phase, i, h], dir_recv.at[phase, i, h], (gz, owner(i)),
        )

    def with_rim(phase, i, h):
        b_rim(phase, i, h).wait_recv()
        inside = jnp.where(h == 0, gz > 0, gz < n_gz - 1)
        return part[phase, i, half(h)] + jnp.where(inside, rim[phase, i, h], 0.0)

    def send_half(phase, i, h):
        part[phase, i, half(h)] = with_rim(phase, i, h)
        b_direct(phase, i, h).start()

    def back(phase, take, beside1=None, beside2=None):
        def product(i, _):
            s = owner(i)
            if phase == 0:
                convert(i, s)
            both = dot(z_both[...], t_hi[s], NN)
            part[phase, i] = both[0:WZ] + (both[WZ:] + dot(z_both[0:WZ], t_lo[s], NN))
            b_rim(phase, i, inner).start()
            b_rim(phase, i, outer).start()

            @pl.when(i > 0)
            def _():
                send_half(phase, i - 1, inner)

            return 0

        lax.fori_loop(0, NCOL, product, 0)
        send_half(phase, 0, outer)
        send_half(phase, 1, outer)
        if beside1 is not None:
            beside1()
        send_half(phase, 2, outer)
        if beside2 is not None:
            beside2()
        for h, far in ((inner, False), (outer, True)):
            own = with_rim(phase, 3, h)
            for i in range(3):
                b_direct(phase, i, h).wait_recv()
            d = [direct[phase, i, half(h, 0)] for i in range(3)]
            take(h, own + (d[0] + (d[1] + d[2])), far)

    def a_main(phase, i, h):
        return remote(
            window.at[phase, 0, half(h)], window.at[phase, i, half(h)],
            gat_send.at[phase, i, h], gat_recv.at[phase, i, h],
            (gz, lax.rem(y + i + lax.div(i, 2) + 2 * lax.div(i, 3), NCOL)),
        )

    def a_rim(phase, i, h, far=False):
        src = window.at[phase, 0 if far else i, half(h)]
        return remote(
            src, window.at[phase, i, edge(h)],
            win_send.at[phase, i, h], win_recv.at[phase, i, h],
            (lax.rem(gz + n_gz - 1 + 2 * h, n_gz), col(2) if far else y),
        )

    def gather_start(phase, h, far):
        a_rim(phase, 0, h).start()
        a_main(phase, 1, h).start()
        a_main(phase, 2, h).start()
        if far:
            a_rim(phase, 3, h, True).start()
        a_main(phase, 3, h).start()

    def gather_product(phase, i):
        s = lax.rem(y + 3 * i + 3 * ((i * (i - 1)) // 2), NCOL)
        low = jnp.where(gz > 0, window[phase, i, 0:HR], 0.0)
        high = jnp.where(gz < n_gz - 1, window[phase, i, WZ - HR : WZ], 0.0)
        hi, lo = split(jnp.concatenate([low, window[phase, i, HR : HR + ZS], high], axis=0))

        value = dot3(t_hi[s], t_lo[s], hi, lo, NT)
        if i == 0:
            q_all[...] = value
        else:
            q_all[...] += value

    def gather(phase, beside0=None, beside1=None, beside2=None):
        def product(i):
            for h in range(2):
                a_rim(phase, i, h).wait_recv()
            gather_product(phase, i)

        def forwards(h):
            for i in (1, 2):
                a_main(phase, i, h).wait_recv()
                a_rim(phase, i, h).start()

        forwards(inner)
        if beside0 is not None:
            beside0()
        forwards(outer)
        a_main(phase, 3, inner).wait_recv()
        a_rim(phase, 3, inner).start()
        product(0)
        if beside1 is not None:
            beside1()
        a_main(phase, 3, outer).wait_recv()
        if beside2 is not None:
            beside2()
        product(3)
        product(1)
        product(2)

    def rays(p):
        hi, lo = split(q_all[pl.ds(pl.multiple_of(p * PW, 128), PW)])

        def one(a, k):
            pick = lambda v: jnp.concatenate(
                [v[k * 128 : (k + 1) * 128], v[256 + k * 64 : 320 + k * 64]], axis=0
            )
            both = dot(pick(hi), jnp.concatenate([w_hi[a], w_lo[a]], axis=1), NN)
            return both[:, :128] + (both[:, 128:] + dot(pick(lo), w_hi[a], NN))

        pa = one(2 * p, 0)
        pb = one(2 * p + 1, 1)
        return jnp.concatenate([pa[:128], pb[:128], pa[128:], pb[128:]], axis=0)

    zero8 = jnp.zeros((8, 128), F32)

    def take_g0(h, value, far):
        g0[half(h, 0)] = value
        window[0, 0, half(h)] = value
        gather_start(0, h, far)

    back(0, take_g0)
    gather(0)

    def rays0(p, acc):
        x = rays(p)
        q0[p] = x
        return acc + squares(x)

    def z_of_rays(q):
        lax.fori_loop(0, PAIRS, lambda p, c: (z_of(p, q[p]), c)[1], 0, unroll=4)

    norm_q0 = lax.fori_loop(0, PAIRS, rays0, zero8, unroll=2)
    ar_first(0, squares(g0[...]), norm_q0)
    z_of_rays(q0)

    def take_h0(h, value, far):
        h0[half(h, 0)] = value
        window[1, 0, half(h)] = value * SCALE
        gather_start(1, h, far)

    back(1, take_h0, beside1=lambda: ar_second(0))

    def step0():
        sums = ar_get(0, 1)
        gamma = total(sums[0:1])
        alpha = gamma / total(sums[1:2])
        scalars[0:1] = jnp.broadcast_to(gamma, (1, 128))
        scalars[1:2] = jnp.broadcast_to(alpha, (1, 128))
        g1[...] = g0[...] - alpha * h0[...]
        ar_first(1, squares(g1[...]), zero8)

    gather(1, step0, None, lambda: ar_second(1))
    gamma0 = scalars[0:1, 0:1]
    alpha0 = scalars[1:2, 0:1]

    def rays1(p, _):
        q1[p] = q0[p] - (alpha0 * (1.0 / SCALE)) * rays(p)
        return 0

    lax.fori_loop(0, PAIRS, rays1, 0, unroll=2)

    gamma1 = total(ar_get(1, 1)[0:1])
    beta = gamma1 / gamma0

    def rays2(p, acc):
        x = q1[p] + beta * q0[p]
        q1[p] = x
        return acc + squares(x)

    ar_first(2, lax.fori_loop(0, PAIRS, rays2, zero8), zero8)
    z_of_rays(q1)

    def take_h1(h, value, _):
        h1[half(h, 0)] = value

    def sent_directs(phase):
        for h in range(2):
            for i in range(3):
                b_direct(phase, i, h).wait_send()

    def sent_earlier():
        for phase in range(2):
            sent_directs(phase)
            for h in range(2):
                for i in range(NCOL):
                    a_rim(phase, i, h).wait_send()
                for i in range(1, NCOL):
                    a_main(phase, i, h).wait_send()
        for phase in range(3):
            for h in range(2):
                for i in range(NCOL):
                    b_rim(phase, i, h).wait_send()

    def residual_parts():
        def some(p, _):
            for at, x0, x1 in zip((early_at(p), late_at(p)), as_measured(q0[p]), as_measured(q1[p])):
                r1[:, at] = meas_ref[:, at] - alpha0 * x0
                res_ref[:, at] = x1
            return 0

        lax.fori_loop(0, PAIRS, some, 0)
        sent_earlier()

    back(2, take_h1, beside1=lambda: ar_second(2), beside2=residual_parts)
    sums = ar_get(2, 1)
    alpha1 = gamma1 / total(sums[0:1])
    grad_ref[...] = g1[...] - alpha1 * h1[...]
    vol_ref[...] = alpha0 * g0[...] + alpha1 * (g1[...] + beta * g0[...])
    res_ref[...] = r1[...] - alpha1 * res_ref[...]

    sent_directs(2)


def hand_on(v_ref, r_ref, g_ref, v_out, r_out, g_out, v, r, g, sem_in, sem_out):
    cut = C // 2 // 8 * 8
    pieces = [(r_ref.at[0:cut], r.at[0:cut], r_out.at[0:cut]), (r_ref.at[cut:], r.at[cut:], r_out.at[cut:])]
    pieces += [(v_ref, v, v_out), (g_ref, g, g_out)]
    ins = [pltpu.make_async_copy(a, b, sem_in.at[k]) for k, (a, b, _) in enumerate(pieces)]
    outs = [pltpu.make_async_copy(b, c, sem_out.at[k]) for k, (_, b, c) in enumerate(pieces)]
    for copy in ins:
        copy.start()
    for arrived, copy in zip(ins, outs):
        arrived.wait()
        copy.start()
    for copy in outs:
        copy.wait()


def on_device(lo_size, measured, view_offset, tile_index, footprint, transaxial):
    hi_size = lax.axis_size("gz") // lo_size
    flat, deep = lo_size // 2 * NCOL, hi_size * 2
    vmem = pl.BlockSpec(memory_space=pltpu.VMEM)
    anywhere = pl.BlockSpec(memory_space=pl.ANY)
    smem = pl.BlockSpec(memory_space=pltpu.SMEM)
    dma = pltpu.SemaphoreType.DMA
    scratch = [
        pltpu.VMEM((NCOL, NA, C, VX), F32),
        pltpu.VMEM((NCOL, KC, VX), BF16),
        pltpu.VMEM((NCOL, KC, VX), BF16),
        pltpu.VMEM((TOP + WZ, 128), F32),
        pltpu.VMEM((NA, WZ, 128), BF16),
        pltpu.VMEM((NA, WZ, 128), BF16),
        pltpu.VMEM((2 * WZ, KC), BF16),
        pltpu.VMEM((KC, WZ), F32),
        pltpu.VMEM((PAIRS, PW, 128), F32),
        pltpu.VMEM((PAIRS, PW, 128), F32),
        pltpu.VMEM((C, 2 * NA * R), F32),
        pltpu.VMEM((3, NCOL, WZ, VX), F32),
        pltpu.VMEM((3, NCOL, 2, HR, VX), F32),
        pltpu.VMEM((3, 3, ZS, VX), F32),
        pltpu.VMEM((2, NCOL, WZ, VX), F32),
        pltpu.VMEM((ZS, VX), F32),
        pltpu.VMEM((ZS, VX), F32),
        pltpu.VMEM((ZS, VX), F32),
        pltpu.VMEM((ZS, VX), F32),
        pltpu.VMEM((8, 128), F32),
        pltpu.VMEM((3, flat, 2, 128), F32),
        pltpu.VMEM((3, deep, 2, 128), F32),
        pltpu.VMEM((C, 2 * NA * R), F32),
        dma(()),
        dma((NCOL,)),
        dma((3, NCOL, 2)),
        dma((3, NCOL, 2)),
        dma((3, 3, 2)),
        dma((3, 3, 2)),
        dma((2, NCOL, 2)),
        dma((2, NCOL, 2)),
        dma((2, NCOL, 2)),
        dma((2, NCOL, 2)),
        dma((3, 2)),
        dma((3, 2)),
    ]
    shapes = (
        jax.ShapeDtypeStruct((ZS, VX), F32),
        jax.ShapeDtypeStruct((C, 2 * NA * R), F32),
        jax.ShapeDtypeStruct((ZS, VX), F32),
    )
    outs = pl.pallas_call(
        functools.partial(kernel, lo_size),
        out_shape=shapes,
        in_specs=[smem, smem, vmem, anywhere, anywhere],
        out_specs=(vmem, vmem, vmem),
        scratch_shapes=scratch,
        compiler_params=pltpu.CompilerParams(
            collective_id=0, has_side_effects=True, vmem_limit_bytes=56 * 1024 * 1024
        ),
        cost_estimate=pl.CostEstimate(flops=12_000_000_000, bytes_accessed=9_000_000, transcendentals=0),
    )(view_offset, tile_index, jnp.swapaxes(footprint, 1, 2), measured, transaxial)
    return pl.pallas_call(
        hand_on,
        out_shape=shapes,
        in_specs=[anywhere] * 3,
        out_specs=(anywhere,) * 3,
        scratch_shapes=[pltpu.VMEM(shape.shape, F32) for shape in shapes] + [dma((4,)), dma((4,))],
        compiler_params=pltpu.CompilerParams(vmem_limit_bytes=60 * 1024 * 1024),
    )(*outs)


def solution(mesh):
    lo_size = min(8, mesh.shape["gz"] // 2)
    return jax.shard_map(
        functools.partial(on_device, lo_size),
        mesh=mesh,
        in_specs=(P("col", "gz"), P("gz"), P("gz"), P(), P(None, "col", None)),
        out_specs=(P("gz", "col"), P("col", "gz"), P("gz", "col")),
        check_vma=False,
    )
```

profile of v0, /device:TPU:1, one launch (start us, length us, event | category | flops | bytes accessed | tf_op | source)
XLA Modules:
  0.0 81.1 jit_solution(4487754258854005037)
XLA Ops:
  0.6 78.4 %shard_map.76 = (f32[128,256]{1,0:T(8,128)}, f32[184,1024]{1,0:T(8,128)}, f32[128,256]{1,0:T(8,128)}) custom-call(s32[16]{0:T(128)} %off_ref.1, s32[16]{0:T(128)} %tile_ref.1, f32[8,32,64]{2,1,0:T(8,128)} %bitcast.1, f32[184,1024]{1,0:T(8,128)} %measured_ref.1, f32[8,184,1024]{2,1,0:T(8,128)} %trans_ref.1), custom_call_target="tpu_custom_call" | custom-call | flops 12000000000 | bytes 9000000 | tf_op jit(solution)/shard_map/pallas_call | solution.py:523
  79.1 2.0 %shard_map.77 = (f32[128,256]{1,0:T(8,128)}, f32[184,1024]{1,0:T(8,128)}, f32[128,256]{1,0:T(8,128)}) custom-call(f32[128,256]{1,0:T(8,128)} %get-tuple-element.6.v_ref, f32[184,1024]{1,0:T(8,128)} %get-tuple-element.7.r_ref, f32[128,256]{1,0:T(8,128)} %get-tuple-element.8.g_ref), custom_call_target="tpu_custom_call" | custom-call | tf_op jit(solution)/shard_map/pallas_call | solution.py:534
where the time goes:
time: 81.2 us; the launch traced here: 81.1 us
  Pallas kernels  80.4 us (99%)
    pallas_call x1, Pallas kernels, on_device(): pl.pallas_call(functools.partial(kernel, lo_size), out_shape=shapes, in_s...  78.4 us
    pallas_call x1, Pallas kernels, on_device(): pl.pallas_call(hand_on, out_shape=shapes, in_specs=[anywhere] * 3, out_sp...  2 us

commit v1 on v0

--- a/solution.py
+++ b/solution.py
@@ -189,8 +189,6 @@
 
         lax.fori_loop(0, PAIRS, some, 0)
 
-    pl.semaphore_wait(barrier, greeted)
-
     def remote(src, dst, send, recv, to):
         return pltpu.make_async_remote_copy(
             src_ref=src, dst_ref=dst, send_sem=send, recv_sem=recv, device_id=to, device_id_type=MESH
@@ -256,8 +254,14 @@
                 convert(i, s)
             both = dot(z_both[...], t_hi[s], NN)
             part[phase, i] = both[0:WZ] + (both[WZ:] + dot(z_both[0:WZ], t_lo[s], NN))
+            if phase == 0:
+
+                @pl.when(i == 0)
+                def _():
+                    pl.semaphore_wait(barrier, greeted)
+
+            b_rim(phase, i, outer).start()
             b_rim(phase, i, inner).start()
-            b_rim(phase, i, outer).start()
 
             @pl.when(i > 0)
             def _():

time: 81.2 us -> 79.6 us (0.980)
  Pallas kernels: 80.4 us -> 78.9 us
    pallas_call x1, Pallas kernels: 78.4 us -> 76.9 us  [on_device(): pl.pallas_call(functools.partial(kernel, lo_size), out_shape=shapes, in_s...]
where the time goes in v1:
time: 79.6 us; the launch traced here: 79.5 us
  Pallas kernels  78.9 us (99%)
    pallas_call x1, Pallas kernels, on_device(): pl.pallas_call(functools.partial(kernel, lo_size), out_shape=shapes, in_s...  76.9 us
    pallas_call x1, Pallas kernels, on_device(): pl.pallas_call(hand_on, out_shape=shapes, in_specs=[anywhere] * 3, out_sp...  2 us

profile of v1, /device:TPU:1, one launch (start us, length us, event | category | flops | bytes accessed | tf_op | source)
XLA Modules:
  0.0 79.5 jit_solution(11951013324721688647)
XLA Ops:
  0.6 76.9 %shard_map.76 = (f32[128,256]{1,0:T(8,128)}, f32[184,1024]{1,0:T(8,128)}, f32[128,256]{1,0:T(8,128)}) custom-call(s32[16]{0:T(128)} %off_ref.1, s32[16]{0:T(128)} %tile_ref.1, f32[8,32,64]{2,1,0:T(8,128)} %bitcast.1, f32[184,1024]{1,0:T(8,128)} %measured_ref.1, f32[8,184,1024]{2,1,0:T(8,128)} %trans_ref.1), custom_call_target="tpu_custom_call" | custom-call | flops 12000000000 | bytes 9000000 | tf_op jit(solution)/shard_map/pallas_call | solution.py:527
  77.5 2.0 %shard_map.77 = (f32[128,256]{1,0:T(8,128)}, f32[184,1024]{1,0:T(8,128)}, f32[128,256]{1,0:T(8,128)}) custom-call(f32[128,256]{1,0:T(8,128)} %get-tuple-element.6.v_ref, f32[184,1024]{1,0:T(8,128)} %get-tuple-element.7.r_ref, f32[128,256]{1,0:T(8,128)} %get-tuple-element.8.g_ref), custom_call_target="tpu_custom_call" | custom-call | tf_op jit(solution)/shard_map/pallas_call | solution.py:538

commit v2 on v1

--- a/solution.py
+++ b/solution.py
@@ -272,9 +272,9 @@
         lax.fori_loop(0, NCOL, product, 0)
         send_half(phase, 0, outer)
         send_half(phase, 1, outer)
+        send_half(phase, 2, outer)
         if beside1 is not None:
             beside1()
-        send_half(phase, 2, outer)
         if beside2 is not None:
             beside2()
         for h, far in ((inner, False), (outer, True)):

time: 79.6 us -> 80.5 us (1.011)
  Pallas kernels: 78.9 us -> 79.8 us
    pallas_call x1, Pallas kernels: 76.9 us -> 77.8 us  [on_device(): pl.pallas_call(functools.partial(kernel, lo_size), out_shape=shapes, in_s...]
where the time goes in v2:
time: 80.5 us; the launch traced here: 80.4 us
  Pallas kernels  79.8 us (99%)
    pallas_call x1, Pallas kernels, on_device(): pl.pallas_call(functools.partial(kernel, lo_size), out_shape=shapes, in_s...  77.8 us
    pallas_call x1, Pallas kernels, on_device(): pl.pallas_call(hand_on, out_shape=shapes, in_specs=[anywhere] * 3, out_sp...  2 us

profile of v2, /device:TPU:1, one launch (start us, length us, event | category | flops | bytes accessed | tf_op | source)
XLA Modules:
  0.0 80.4 jit_solution(5553125392252584165)
XLA Ops:
  0.6 77.8 %shard_map.76 = (f32[128,256]{1,0:T(8,128)}, f32[184,1024]{1,0:T(8,128)}, f32[128,256]{1,0:T(8,128)}) custom-call(s32[16]{0:T(128)} %off_ref.1, s32[16]{0:T(128)} %tile_ref.1, f32[8,32,64]{2,1,0:T(8,128)} %bitcast.1, f32[184,1024]{1,0:T(8,128)} %measured_ref.1, f32[8,184,1024]{2,1,0:T(8,128)} %trans_ref.1), custom_call_target="tpu_custom_call" | custom-call | flops 12000000000 | bytes 9000000 | tf_op jit(solution)/shard_map/pallas_call | solution.py:527
  78.4 2.0 %shard_map.77 = (f32[128,256]{1,0:T(8,128)}, f32[184,1024]{1,0:T(8,128)}, f32[128,256]{1,0:T(8,128)}) custom-call(f32[128,256]{1,0:T(8,128)} %get-tuple-element.6.v_ref, f32[184,1024]{1,0:T(8,128)} %get-tuple-element.7.r_ref, f32[128,256]{1,0:T(8,128)} %get-tuple-element.8.g_ref), custom_call_target="tpu_custom_call" | custom-call | tf_op jit(solution)/shard_map/pallas_call | solution.py:538
